TPU v7x, 32 devices: a whole 2x2x4 slice. The times are simulated.
32 devices in a mesh: ctx: 8 (over y, x, core), head: 4 (over z).
Axes of the slice: x: 2, y: 2, z: 4, core: 2. Of those that a mesh axis runs over, the one named last changes fastest.
Arguments:
- hidden_in: bfloat16 [1024, 4096], P('ctx', 'head'), may hold values from -6 to 6
- queries: bfloat16 [1024, 4096], P('ctx', 'head'), may hold values from -16 to 16
- kv_prev: bfloat16 [1024, 2, 4096], P('ctx', None, 'head'), may hold values from -16 to 16
- norm_gain: bfloat16 [4096], replicated, may hold values from 0.099609375 to 1.8984375
- w_kv: bfloat16 [4096, 2, 4096], P(None, None, 'head'), may hold values from -0.09375 to 0.09375
- w_out: bfloat16 [4096, 4096], P('head', 'ctx'), may hold values from -0.1875 to 0.1875
Outputs:
- hidden_out: float32 [1024, 4096], P('ctx', 'head')
- kv_out: float32 [1024, 2, 4096], P('ctx', None, 'head')
All inputs are finite; a program needn't handle non-finite values.
Results may differ from a plain program's by a relative error of at most 0.033.
Values may be sent and summed in bfloat16 or wider, within the bound.
A program may use at most 128 MiB of HBM per device.

v0:
```python
import jax
import jax.numpy as jnp
from jax import lax
from jax.sharding import PartitionSpec as P

HD = 128
ITERS = 2


MASKED = -1e30
EPSILON = 1e-05


def attend_keys(query_heads, key_value, row_start):
    row_count = query_heads.shape[0]
    head_count = query_heads.shape[1]
    score_scale = HD ** (-0.5)
    query_position = row_start + jnp.arange(row_count)
    row_last = row_start + row_count - 1
    initial = (
        jnp.full((row_count, head_count), MASKED, jnp.float32),
        jnp.zeros((row_count, head_count), jnp.float32),
        jnp.zeros((row_count, head_count, HD), jnp.float32),
    )
    incoming = lax.all_gather(key_value, "ctx", axis=0, tiled=True)

    def advance(current):
        row_max, row_sum, weighted = current
        block_rows = incoming.shape[0]
        key_block = incoming[:, 0].reshape(block_rows, head_count, HD)
        value_block = incoming[:, 1].reshape(block_rows, head_count, HD)
        scores = (
            jnp.einsum("qhd,khd->qhk", query_heads, key_block, preferred_element_type=jnp.float32)
            * score_scale
        )
        allowed = (query_position[:, None] >= jnp.arange(block_rows)[None, :])[:, None, :]
        scores = jnp.where(allowed, scores, MASKED)
        new_max = jnp.maximum(row_max, jnp.max(scores, axis=2))
        weights = jnp.where(allowed, jnp.exp(scores - new_max[:, :, None]), 0.0)
        row_sum = jnp.sum(weights, axis=2)
        weighted = jnp.einsum(
            "qhk,khd->qhd",
            weights.astype(jnp.bfloat16),
            value_block,
            preferred_element_type=jnp.float32,
        )
        return (new_max, row_sum, weighted)

    row_max, row_sum, weighted = lax.cond(
        jnp.int32(0) <= row_last, advance, lambda current: current, initial
    )
    return (weighted / row_sum[:, :, None]).astype(jnp.bfloat16).reshape(row_count, head_count * HD)


def per_device(hidden_in, queries, kv_prev, norm_gain, w_kv, w_out):
    row_count = queries.shape[0]
    local_width = queries.shape[1]
    head_count = local_width // HD
    row_start = lax.axis_index("ctx") * row_count
    column_start = lax.axis_index("head") * local_width
    out_rows = lax.all_gather(w_out, "ctx", axis=1, tiled=True)
    kv_weights = w_kv.reshape(w_kv.shape[0], 2 * local_width)
    gain_all = norm_gain.astype(jnp.float32)
    query_heads = queries.reshape(row_count, head_count, HD)
    input_all = lax.all_gather(hidden_in, "head", axis=1, tiled=True).astype(jnp.float32)
    key_value = kv_prev
    for iteration in range(ITERS):
        attended = attend_keys(query_heads, key_value, row_start)
        partial_value = jnp.dot(attended, out_rows, preferred_element_type=jnp.float32)
        branch_sum = lax.psum(partial_value.astype(jnp.bfloat16), "head").astype(jnp.float32)
        hidden = input_all + branch_sum
        mean_square = jnp.mean(hidden * hidden, axis=1, keepdims=True)
        normed = (hidden * lax.rsqrt(mean_square + EPSILON) * gain_all).astype(jnp.bfloat16)
        fresh_kv = jnp.dot(normed, kv_weights, preferred_element_type=jnp.float32)
        hidden_out = lax.dynamic_slice_in_dim(hidden, column_start, local_width, 1)
        kv_product = fresh_kv.reshape(row_count, 2, local_width)
        key_value = kv_product.astype(jnp.bfloat16)
    return (hidden_out, kv_product)


def solution(mesh):
    in_specs = (
        P("ctx", "head"),
        P("ctx", "head"),
        P("ctx", None, "head"),
        P(),
        P(None, None, "head"),
        P("head", "ctx"),
    )
    out_specs = (P("ctx", "head"), P("ctx", None, "head"))
    return jax.shard_map(
        per_device, mesh=mesh, in_specs=in_specs, out_specs=out_specs, check_vma=False
    )
```

profile of v0, /device:TPU:0, one launch (start us, length us, event | category | flops | bytes accessed | tf_op | source)
XLA Modules:
  0.0 339.1 jit_solution(10983850110053488918)
XLA Ops:
  7.2 0.0 all-gather.7.cloned.1.call-start
  7.2 2.0 copy.38
  9.2 0.0 all-gather.7.cloned.1.call-update
  9.2 0.0 all-gather.9.cloned.1.call-start
  9.3 0.7 all-gather.9.cloned.1.call-update
  10.0 0.0 all-gather.5.cloned.1.call-start
  10.0 0.7 all-gather.5.cloned.1.call-update
  10.7 0.0 all-reduce.3.cloned.1.call-start
  10.8 1.1 copy.39
  11.9 38.7 %all-gather.7.cloned.1.call-done = bf16[1024,2,1024]{0,2,1:T(8,128)(2,1)} async-done(((bf16[128,2,1024]{0,2,1:T(8,128)(2,1)}), bf16[1024,2,1024]{0,2,1:T(8,128)(2,1)}) %all-gather.7.cloned.1.call-update) | async-done | bytes 4194320 | tf_op jit(solution)/shard_map/all_gather | solution.py:25
  50.6 6.7 %conditional.2 = (f32[128,8]{0,1:T(8,128)S(1)}, f32[128,8,128]{0,2,1:T(8,128)S(1)}) conditional(s32[]{:T(128)} %convert_element_type.44, () %tuple.25, (s32[128]{0:T(128)S(1)}, bf16[1024,2,1024]{0,2,1:T(8,128)(2,1)}, bf16[128,8,128]{0,2,1:T(8,128)(2,1)S(1)}) %tuple.62), branch_computations={%region_0.0_spmd, %region_1.4_spmd} | conditional | flops 550632448 | bytes 27550224 | solution.py:49
  50.6 0.1 iota_compare_fusion
  50.7 2.7 fusion.41
  53.4 1.1 fusion
  54.5 1.0 fusion.2
  55.6 1.6 fusion.10
  57.1 0.2 copy.56
  57.3 0.1 divide_convert_fusion.1
  57.4 51.1 %all-gather.9.cloned.1.call-done = bf16[1024,4096]{1,0:T(8,128)(2,1)} async-done(((bf16[1024,512]{1,0:T(8,128)(2,1)}), bf16[1024,4096]{1,0:T(8,128)(2,1)}) %all-gather.9.cloned.1.call-update) | async-done | bytes 8388624 | tf_op jit(solution)/shard_map/all_gather | solution.py:61
  108.5 5.6 %convolution_convert_fusion.1 = bf16[128,4096]{1,0:T(8,128)(2,1)} fusion(bf16[128,1024]{0,1:T(8,128)(2,1)S(1)} %bitcast.70, bf16[1024,4096]{1,0:T(8,128)(2,1)} %all-gather.9.cloned.1.call-done), kind=kOutput, calls=%fused_computation.35 | convolution fusion | flops 1074266112 | bytes 9699328 | tf_op jit(solution)/shard_map/dot_general | solution.py:69
  114.1 0.0 all-reduce.3.cloned.1.call-update
  114.1 0.2 all-gather.11.cloned.1.call-start
  114.4 17.1 %copy.59 = bf16[512,8,2,1024]{3,1,2,0:T(8,128)(2,1)} copy(bf16[512,8,2,1024]{3,2,1,0:T(2,128)(2,1)} %bitcast.63) | data formatting | bytes 33554432
  131.5 21.0 %copy.42 = bf16[2048,4096]{1,0:T(8,128)(2,1)} copy(bf16[2048,4096]{0,1:T(8,128)(2,1)} %bitcast.62) | data formatting | bytes 33554432 | tf_op jit(solution)/shard_map/dot_general | solution.py:74
  152.5 0.0 all-gather.5.cloned.1.call-done
  152.5 39.7 %all-reduce.3.cloned.1.call-done = bf16[128,4096]{1,0:T(8,128)(2,1)} async-done(((bf16[128,4096]{1,0:T(8,128)(2,1)}), bf16[128,4096]{1,0:T(8,128)(2,1)}) %all-reduce.3.cloned.1.call-update) | async-done | bytes 1048592 | tf_op jit(solution)/shard_map/psum | solution.py:70
  192.2 2.0 multiply_reduce_fusion.1
  194.2 12.9 %convolution_convert_fusion.2 = bf16[128,2,1024]{2,0,1:T(8,128)(2,1)} fusion(bf16[2,1024,4096]{2,1,0:T(8,128)(2,1)} %bitcast.60, bf16[128,4096]{1,0:T(8,128)(2,1)} %all-reduce.3.cloned.1.call-done, bf16[128,4096]{1,0:T(8,128)(2,1)} %all-gather.5.cloned.1.call-done, f32[4096]{0:T(1024)S(1)} %convert_element_type.48, f32[128]{0:T(128)S(1)} %add_rsqrt_fusion.1), kind=kOutput, calls=%fused_computation.42 | convolution fusion | flops 2150891520 | bytes 19415552 | tf_op jit(solution)/shard_map/dot_general | solution.py:74
  207.0 0.0 all-gather.11.cloned.1.call-update
  207.1 0.3 all-reduce.5.cloned.1.call-start
  207.3 36.0 %all-gather.11.cloned.1.call-done = bf16[1024,2,1024]{2,0,1:T(8,128)(2,1)} async-done(((bf16[128,2,1024]{2,0,1:T(8,128)(2,1)}), bf16[1024,2,1024]{2,0,1:T(8,128)(2,1)}) %all-gather.11.cloned.1.call-update) | async-done | bytes 4194320 | tf_op jit(solution)/shard_map/all_gather | solution.py:25
  243.3 13.0 %conditional.3 = (f32[128,8]{0,1:T(8,128)S(1)}, f32[128,8,128]{0,2,1:T(8,128)S(1)}) conditional(s32[]{:T(128)} %convert_element_type.44, () %tuple.24, (s32[128]{0:T(128)S(1)}, bf16[1024,2,1024]{2,0,1:T(8,128)(2,1)}, bf16[128,8,128]{0,2,1:T(8,128)(2,1)S(1)}) %tuple.63), branch_computations={%region_6.7_spmd, %region_7.10_spmd} | conditional | flops 550632448 | bytes 35938832 | solution.py:49
  243.3 0.1 iota_compare_fusion.1
  243.4 6.3 %copy.43 = bf16[1024,2,1024]{0,2,1:T(8,128)(2,1)} copy(bf16[1024,2,1024]{2,0,1:T(8,128)(2,1)} %get-tuple-element.45) | data formatting | bytes 8388608 | tf_op jit(solution)/shard_map
  249.7 2.7 fusion.42
  252.3 1.1 fusion.16
  253.5 1.0 fusion.18
  254.5 1.6 fusion.26
  256.1 0.2 copy.58
  256.3 0.1 divide_convert_fusion
  256.4 0.0 copy-start
  256.4 5.7 %convolution_convert_fusion = bf16[128,4096]{1,0:T(8,128)(2,1)} fusion(bf16[128,1024]{0,1:T(8,128)(2,1)S(1)} %bitcast.71, bf16[1024,4096]{1,0:T(8,128)(2,1)} %all-gather.9.cloned.1.call-done), kind=kOutput, calls=%fused_computation.34 | convolution fusion | flops 1074266112 | bytes 9699328 | tf_op jit(solution)/shard_map/dot_general | solution.py:69
  262.1 0.0 all-reduce.5.cloned.1.call-update
  262.1 52.0 %all-reduce.5.cloned.1.call-done = bf16[128,4096]{1,0:T(8,128)(2,1)} async-done(((bf16[128,4096]{1,0:T(8,128)(2,1)}), bf16[128,4096]{1,0:T(8,128)(2,1)}) %all-reduce.5.cloned.1.call-update) | async-done | bytes 1048592 | tf_op jit(solution)/shard_map/psum | solution.py:70
  314.1 3.0 multiply_reduce_fusion
  317.1 11.4 %fusion.35 = f32[128,2,1024]{2,0,1:T(8,128)S(1)} fusion(bf16[2,1024,4096]{2,1,0:T(8,128)(2,1)} %bitcast.61, f32[128]{0:T(128)S(1)} %add_rsqrt_fusion, f32[4096]{0:T(1024)S(1)} %convert_element_type.48, bf16[128,4096]{1,0:T(8,128)(2,1)S(1)} %copy-done, bf16[128,4096]{1,0:T(8,128)(2,1)S(1)} %copy-done.1), kind=kOutput, calls=%fused_computation.45 | convolution fusion | flops 2150629376 | bytes 19939840 | tf_op jit(solution)/shard_map/dot_general | solution.py:74
  328.6 1.8 copy.46
  330.3 1.9 constant_dynamic-slice_fusion
  (11 shorter events, 0.0 us)
Async XLA Ops:
  7.2 43.5 %all-gather.7.cloned.1.call-start = ((), (), s32[]{:S(2)}) async-start(), calls=%async_computation.1 | async-start | bytes 4718592 | tf_op jit(solution)/shard_map/all_gather | solution.py:25
  9.2 99.2 %all-gather.9.cloned.1.call-start = ((), (), s32[]{:S(2)}) async-start(), calls=%async_computation.2 | async-start | bytes 9437184 | tf_op jit(solution)/shard_map/all_gather | solution.py:61
  10.0 142.5 %all-gather.5.cloned.1.call-start = ((), (), s32[]{:S(2)}) async-start(), calls=%async_computation | async-start | bytes 1310720 | tf_op jit(solution)/shard_map/all_gather | solution.py:65
  10.7 181.4 %all-reduce.3.cloned.1.call-start = ((), (), s32[]{:S(2)}) async-start(), calls=%async_computation.3 | async-start | bytes 2097152 | tf_op jit(solution)/shard_map/psum | solution.py:70
  114.1 129.2 %all-gather.11.cloned.1.call-start = ((), (), s32[]{:S(2)}) async-start(), calls=%async_computation.4 | async-start | bytes 4718592 | tf_op jit(solution)/shard_map/all_gather | solution.py:25
  131.5 21.0 %copy-start.2 = (bf16[4096]{0:T(1024)(128)(2,1)S(1)}, bf16[4096]{0:T(1024)(128)(2,1)}, u32[]{:S(2)}) copy-start(bf16[4096]{0:T(1024)(128)(2,1)} %param.13) | copy-start | bytes 24580
  207.1 107.0 %all-reduce.5.cloned.1.call-start = ((), (), s32[]{:S(2)}) async-start(), calls=%async_computation.5 | async-start | bytes 2097152 | tf_op jit(solution)/shard_map/psum | solution.py:70
  256.4 57.7 %copy-start = (bf16[128,4096]{1,0:T(8,128)(2,1)S(1)}, bf16[128,4096]{1,0:T(8,128)(2,1)}, u32[]{:S(2)}) copy-start(bf16[128,4096]{1,0:T(8,128)(2,1)} %all-gather.5.cloned.1.call-done) | copy-start | bytes 3145732
  314.1 3.0 copy-start.1
Sparse Core Ops, SparseCore 0:
  10.4 40.1 all-gather.6
  52.5 55.9 all-gather.8
  110.1 27.9 all-gather.4
  140.8 51.3 all-reduce.2
  207.2 36.0 all-gather.10
  262.2 51.7 all-reduce.4
where the time goes:
time: 340 us; the launch traced here: 339 us
  waiting for transfers between devices  219 us (64%)
  local copies, waits for them, and re-layouts  56.9 us (17%)
  matrix products  41.1 us (12%)
  between operations  14.2 us (4%)
  other arithmetic  7.32 us (2%)
    psum x2, waiting for transfers between devices, per_device(): lax.psum(partial_value.astype(jnp.bfloat16), 'head').astype(jnp.float32)  91.7 us
    all_gather x2, waiting for transfers between devices, attend_keys(): incoming = lax.all_gather(key_value, 'ctx', axis=0, tiled=True)  74.7 us
    all_gather x1, waiting for transfers between devices, per_device(): out_rows = lax.all_gather(w_out, 'ctx', axis=1, tiled=True)  51.1 us
    dot_general x2, matrix products, per_device(): fresh_kv = jnp.dot(normed, kv_weights, preferred_element_type=jnp.float32)  24.3 us
    unnamed x10, local copies, waits for them, and re-layouts  22 us
    dot_general x1, local copies, waits for them, and re-layouts, per_device(): fresh_kv = jnp.dot(normed, kv_weights, preferred_element_type=jnp.float32)  21 us
    dot_general x2, matrix products, per_device(): jnp.dot(attended, out_rows, preferred_element_type=jnp.float32)  11.4 us
  transfers between devices with their start and end apart: 6, of which 5 were waited for; matrix products, arithmetic and copies ran while one was open for 15% of the time, Pallas kernels for 0%

commit v1 on v0

v1 whole, which is shorter than its diff:
```python
import functools

import jax
import jax.numpy as jnp
from jax import lax
from jax.experimental import pallas as pl
from jax.experimental.pallas import tpu as pltpu
from jax.sharding import PartitionSpec as P

HD = 128
ITERS = 2
CORES = 2

MASKED = -1e30
EPSILON = 1e-05
MESH = pl.DeviceIdType.MESH


def attend_block(query, keys, values, row_start):
    scores = lax.dot_general(
        query, keys, (((1,), (1,)), ((), ())), preferred_element_type=jnp.float32
    ) * (HD ** (-0.5))
    rows = row_start + lax.broadcasted_iota(jnp.int32, scores.shape, 0)
    columns = lax.broadcasted_iota(jnp.int32, scores.shape, 1)
    scores = jnp.where(rows >= columns, scores, MASKED)
    weights = jnp.exp(scores - jnp.max(scores, axis=1, keepdims=True))
    row_sum = jnp.sum(weights, axis=1, keepdims=True)
    weighted = jnp.dot(weights.astype(jnp.bfloat16), values, preferred_element_type=jnp.float32)
    return (weighted / row_sum).astype(jnp.bfloat16)


def fused_kernel(
    n, zn, q_ref, k_ref, v_ref, hin_ref, gain_ref, wout_ref, wkv_hbm, hid_ref, kvo_ref,
    qkv, kv_next, w_pair, hin_all, a_send, a_all, p_send, rs, b_send, b_all, normed, kv_send, wkv,
    load_sem, local_sem, pair_send, pair_recv, in_send, in_recv, hin_send, hin_recv,
    a_ssem, a_rsem, p_ssem, p_rsem, b_ssem, b_rsem, g_ssem, g_rsem, kv_ssem, kv_rsem,
):
    c = lax.axis_index("ctx")
    z = lax.axis_index("head")
    core = lax.rem(c, CORES)
    k = lax.div(c, CORES)
    groups = n // CORES
    rows, width = q_ref.shape
    quarter = rows // zn
    block = rows * CORES
    chip_width = CORES * wout_ref.shape[1]
    pending = []

    def send(src, dst, ssem, rsem, where):
        copy = pltpu.make_async_remote_copy(
            src_ref=src, dst_ref=dst, send_sem=ssem, recv_sem=rsem, device_id=where, device_id_type=MESH
        )
        copy.start()
        pending.append(copy)
        return copy

    def cols(index, size):
        return pl.ds(pl.multiple_of(index * size, size), size)

    load = pltpu.make_async_copy(wkv_hbm, wkv, load_sem)
    load.start()
    own_w = pltpu.make_async_copy(wout_ref, w_pair.at[core], local_sem)
    own_w.start()

    barrier = pltpu.get_barrier_semaphore()
    for d in range(1, n):
        pl.semaphore_signal(barrier, inc=1, device_id={"ctx": lax.rem(c + d, n)}, device_id_type=MESH)
    for d in range(1, zn):
        pl.semaphore_signal(barrier, inc=1, device_id={"head": lax.rem(z + d, zn)}, device_id_type=MESH)
    pl.semaphore_wait(barrier, n - 1 + zn - 1)

    arrivals = []
    for kind, ref in ((1, k_ref), (0, q_ref), (2, v_ref)):
        for d in range(1, n):
            peer = lax.rem(c + d, n)
            arrivals.append(send(
                ref.at[:, cols(peer, HD)], qkv.at[kind, cols(c, rows)],
                in_send.at[kind, d], in_recv.at[kind, d], {"ctx": peer},
            ))
        qkv[kind, cols(c, rows), :] = ref[:, cols(c, HD)]
    pair = send(wout_ref, w_pair.at[core], pair_send, pair_recv, {"ctx": k * CORES + 1 - core})
    hin_copies = [
        send(hin_ref, hin_all.at[:, cols(z, width)], hin_send.at[d], hin_recv.at[d],
             {"head": lax.rem(z + d, zn)})
        for d in range(1, zn)
    ]
    hin_all[:, cols(z, width)] = hin_ref[...]

    for it in range(ITERS):
        for copy in arrivals:
            copy.wait_recv()
        key_ref = qkv.at[1] if it == 0 else kv_next.at[0]
        value_ref = qkv.at[2] if it == 0 else kv_next.at[1]

        a_copies = []
        for i in range(groups):
            limit = (i + 1) * block
            attended = attend_block(
                qkv[0, i * block:limit, :], key_ref[0:limit, :], value_ref[0:limit, :], i * block
            )
            for side in range(CORES):
                a_send[it, i, side] = attended[side * rows:(side + 1) * rows, :]
            for d in range(1, n):
                peer = lax.rem(c + d, n)
                a_copies.append(send(
                    a_send.at[it, i, lax.rem(peer, CORES)], a_all.at[it, i, :, cols(c, HD)],
                    a_ssem.at[it, i, d], a_rsem.at[it, i, d], {"ctx": peer},
                ))
            a_all[it, i, :, cols(c, HD)] = a_send[it, i, core]
        if it == 0:
            own_w.wait()
            pair.wait_recv()
        for copy in a_copies:
            copy.wait_recv()

        p_copies = []
        for t in range(groups):
            i = lax.rem(k + 1 + t, groups)
            half = chip_width // CORES
            for side in range(CORES):
                product = jnp.dot(
                    a_all[it, i], w_pair[side], preferred_element_type=jnp.float32
                ).astype(jnp.bfloat16)
                for s in range(zn):
                    p_send[it, i, s, :, side * half:(side + 1) * half] = product[s * quarter:(s + 1) * quarter, :]
            for d in range(1, zn):
                target = lax.rem(z + d, zn)
                p_copies.append(send(
                    p_send.at[it, i, target], rs.at[it, d - 1, i],
                    p_ssem.at[it, t, d], p_rsem.at[it, t, d], {"head": target},
                ))

        b_copies = []
        for t in range(groups):
            i = lax.rem(k + 1 + t, groups)
            total = p_send[it, i, z].astype(jnp.float32)
            for d in range(1, zn):
                p_copies[t * (zn - 1) + d - 1].wait_recv()
                total = total + rs[it, d - 1, i].astype(jnp.float32)
            total = total.astype(jnp.bfloat16)
            if t == groups - 1:
                b_all[it, z, :, cols(k, chip_width)] = total
            else:
                b_send[it, t] = total
                b_copies.append(send(
                    b_send.at[it, t], b_all.at[it, z, :, cols(k, chip_width)],
                    b_ssem.at[it, t], b_rsem.at[it, t], {"ctx": i * CORES + core},
                ))

        g_copies = []
        for t in range(groups):
            source = lax.rem(k + groups - 1 - t, groups)
            if t < groups - 1:
                b_copies[t].wait_recv()
            for d in range(1, zn):
                place = b_all.at[it, z, :, cols(source, chip_width)]
                g_copies.append(send(
                    place, place, g_ssem.at[it, t, d], g_rsem.at[it, t, d], {"head": lax.rem(z + d, zn)}
                ))
        if it == 0:
            for copy in hin_copies:
                copy.wait_recv()
        for d in range(zn):
            part = lax.rem(z + zn - d, zn)
            if d > 0:
                for t in range(groups):
                    g_copies[t * (zn - 1) + d - 1].wait_recv()
            span = cols(part, quarter)
            hidden = hin_all[span, :].astype(jnp.float32) + b_all[it, part].astype(jnp.float32)
            mean_square = jnp.mean(hidden * hidden, axis=1, keepdims=True)
            normed[span, :] = (
                hidden * lax.rsqrt(mean_square + EPSILON) * gain_ref[...].astype(jnp.float32)
            ).astype(jnp.bfloat16)
            if it == ITERS - 1:
                hid_ref[span, :] = hin_ref[span, :].astype(jnp.float32) + b_all[
                    it, part, :, cols(z, width)
                ].astype(jnp.float32)

        if it == 0:
            load.wait()
        arrivals = []
        for kind in range(2):
            @pl.loop(0, width // 256)
            def _(j):
                product = jnp.dot(
                    normed[...], wkv[kind, :, cols(j, 256)], preferred_element_type=jnp.float32
                )
                if it == ITERS - 1:
                    kvo_ref[kind, :, cols(j, 256)] = product
                else:
                    kv_send[kind, :, cols(j, 256)] = product.astype(jnp.bfloat16)

            if it < ITERS - 1:
                for d in range(1, n):
                    peer = lax.rem(c + d, n)
                    arrivals.append(send(
                        kv_send.at[kind, :, cols(peer, HD)], kv_next.at[kind, cols(c, rows)],
                        kv_ssem.at[kind, d], kv_rsem.at[kind, d], {"ctx": peer},
                    ))
                kv_next[kind, cols(c, rows), :] = kv_send[kind, :, cols(c, HD)]

    for copy in pending:
        copy.wait_send()


def fused_device(n, zn, hidden_in, queries, kv_prev, norm_gain, w_kv, w_out):
    rows, width = queries.shape
    model = w_kv.shape[0]
    tokens = rows * n
    groups = n // CORES
    quarter = rows // zn
    chip_width = CORES * w_out.shape[1]
    vmem = pl.BlockSpec(memory_space=pltpu.VMEM)
    bf16 = jnp.bfloat16
    dma = pltpu.SemaphoreType.DMA
    hidden_out, kv = pl.pallas_call(
        functools.partial(fused_kernel, n, zn),
        out_shape=(
            jax.ShapeDtypeStruct((rows, width), jnp.float32),
            jax.ShapeDtypeStruct((2, rows, width), jnp.float32),
        ),
        in_specs=[vmem] * 6 + [pl.BlockSpec(memory_space=pl.ANY)],
        out_specs=(vmem, vmem),
        scratch_shapes=[
            pltpu.VMEM((3, tokens, HD), bf16),
            pltpu.VMEM((2, tokens, HD), bf16),
            pltpu.VMEM((CORES,) + w_out.shape, bf16),
            pltpu.VMEM((rows, model), bf16),
            pltpu.VMEM((ITERS, groups, CORES, rows, HD), bf16),
            pltpu.VMEM((ITERS, groups, rows, width), bf16),
            pltpu.VMEM((ITERS, groups, zn, quarter, chip_width), bf16),
            pltpu.VMEM((ITERS, zn - 1, groups, quarter, chip_width), bf16),
            pltpu.VMEM((ITERS, groups - 1, quarter, chip_width), bf16),
            pltpu.VMEM((ITERS, zn, quarter, model), bf16),
            pltpu.VMEM((rows, model), bf16),
            pltpu.VMEM((2, rows, width), bf16),
            pltpu.VMEM((2, model, width), bf16),
            dma, dma, dma, dma,
            dma((3, n)), dma((3, n)),
            dma((zn,)), dma((zn,)),
            dma((ITERS, groups, n)), dma((ITERS, groups, n)),
            dma((ITERS, groups, zn)), dma((ITERS, groups, zn)),
            dma((ITERS, groups)), dma((ITERS, groups)),
            dma((ITERS, groups, zn)), dma((ITERS, groups, zn)),
            dma((2, n)), dma((2, n)),
        ],
        compiler_params=pltpu.CompilerParams(
            collective_id=0, has_side_effects=True, vmem_limit_bytes=56 * 1024 * 1024
        ),
    )(
        queries, kv_prev[:, 0], kv_prev[:, 1], hidden_in, norm_gain.reshape(1, model), w_out,
        w_kv.transpose(1, 0, 2),
    )
    return hidden_out, kv.transpose(1, 0, 2)


def attend_gathered(query_heads, key_value, row_start):
    row_count, head_count = query_heads.shape[:2]
    incoming = lax.all_gather(key_value, "ctx", axis=0, tiled=True)
    block_rows = incoming.shape[0]
    key_block = incoming[:, 0].reshape(block_rows, head_count, HD)
    value_block = incoming[:, 1].reshape(block_rows, head_count, HD)
    scores = (
        jnp.einsum("qhd,khd->qhk", query_heads, key_block, preferred_element_type=jnp.float32)
        * HD ** (-0.5)
    )
    positions = row_start + jnp.arange(row_count)
    allowed = (positions[:, None] >= jnp.arange(block_rows)[None, :])[:, None, :]
    scores = jnp.where(allowed, scores, MASKED)
    weights = jnp.where(allowed, jnp.exp(scores - jnp.max(scores, axis=2, keepdims=True)), 0.0)
    row_sum = jnp.sum(weights, axis=2)
    weighted = jnp.einsum(
        "qhk,khd->qhd", weights.astype(jnp.bfloat16), value_block, preferred_element_type=jnp.float32
    )
    return (weighted / row_sum[:, :, None]).astype(jnp.bfloat16).reshape(row_count, head_count * HD)


def gathered_device(hidden_in, queries, kv_prev, norm_gain, w_kv, w_out):
    row_count, local_width = queries.shape
    head_count = local_width // HD
    row_start = lax.axis_index("ctx") * row_count
    column_start = lax.axis_index("head") * local_width
    out_rows = lax.all_gather(w_out, "ctx", axis=1, tiled=True)
    kv_weights = w_kv.reshape(w_kv.shape[0], 2 * local_width)
    gain_all = norm_gain.astype(jnp.float32)
    query_heads = queries.reshape(row_count, head_count, HD)
    input_all = lax.all_gather(hidden_in, "head", axis=1, tiled=True).astype(jnp.float32)
    key_value = kv_prev
    for _ in range(ITERS):
        attended = attend_gathered(query_heads, key_value, row_start)
        partial_value = jnp.dot(attended, out_rows, preferred_element_type=jnp.float32)
        branch_sum = lax.psum(partial_value.astype(jnp.bfloat16), "head").astype(jnp.float32)
        hidden = input_all + branch_sum
        mean_square = jnp.mean(hidden * hidden, axis=1, keepdims=True)
        normed = (hidden * lax.rsqrt(mean_square + EPSILON) * gain_all).astype(jnp.bfloat16)
        fresh_kv = jnp.dot(normed, kv_weights, preferred_element_type=jnp.float32)
        hidden_out = lax.dynamic_slice_in_dim(hidden, column_start, local_width, 1)
        kv_product = fresh_kv.reshape(row_count, 2, local_width)
        key_value = kv_product.astype(jnp.bfloat16)
    return (hidden_out, kv_product)


def per_device(n, zn, *args):
    rows, width = args[1].shape
    if width == n * HD and n % CORES == 0 and rows % (16 * zn) == 0 and zn > 1:
        return fused_device(n, zn, *args)
    return gathered_device(*args)


def solution(mesh):
    in_specs = (
        P("ctx", "head"),
        P("ctx", "head"),
        P("ctx", None, "head"),
        P(),
        P(None, None, "head"),
        P("head", "ctx"),
    )
    out_specs = (P("ctx", "head"), P("ctx", None, "head"))
    return jax.shard_map(
        functools.partial(per_device, mesh.shape["ctx"], mesh.shape["head"]),
        mesh=mesh, in_specs=in_specs, out_specs=out_specs, check_vma=False,
    )
```

time: 340 us -> 185 us (0.54)
  waiting for transfers between devices: 219 us -> 0 us
  Pallas kernels: 0 us -> 158 us
  matrix products: 41.1 us -> 0 us
  local copies, waits for them, and re-layouts: 56.9 us -> 25.7 us
  between operations: 14.2 us -> 0.64 us
  other arithmetic: 7.32 us -> 0 us
    pallas_call x0 -> x1, Pallas kernels: none -> 158 us  [fused_device(): pl.pallas_call(functools.partial(fused_kernel, n, zn), out_shape=(jax.Sha...]
    all_gather x4 -> x0, waiting for transfers between devices: 126 us -> none  [the longest x2 74.7 us: attend_keys(): incoming = lax.all_gather(key_value, 'ctx', axis=0, tiled=True)]
    psum x2 -> x0, waiting for transfers between devices: 91.7 us -> none  [per_device(): lax.psum(partial_value.astype(jnp.bfloat16), 'head').astype(jnp.float32)]
    dot_general x8 -> x0, matrix products: 41.1 us -> none  [the longest x2 24.3 us: per_device(): fresh_kv = jnp.dot(normed, kv_weights, preferred_element_type=jnp.float32)]
    dot_general x1 -> x0, local copies, waits for them, and re-layouts: 21 us -> none  [per_device(): fresh_kv = jnp.dot(normed, kv_weights, preferred_element_type=jnp.float32)]
    reduce_sum x4 -> x0, other arithmetic: 7 us -> none  [the longest x2 4.97 us: per_device(): mean_square = jnp.mean(hidden * hidden, axis=1, keepdims=True)]
    another operation x1 -> x0, local copies, waits for them, and re-layouts: 6.26 us -> none
    unnamed x10 -> x3, local copies, waits for them, and re-layouts: 22 us -> 21.3 us
  transfers between devices with their start and end apart: 6 -> 0, of which waited for: 5 -> 0; matrix products, arithmetic and copies ran while one was open for 15% -> 0% of each run, Pallas kernels for 0% -> 0%
where the time goes in v1:
time: 185 us
  Pallas kernels  158 us (85%)
  local copies, waits for them, and re-layouts  25.7 us (14%)
    pallas_call x1, Pallas kernels, fused_device(): pl.pallas_call(functools.partial(fused_kernel, n, zn), out_shape=(jax.Sha...  158 us
    unnamed x3, local copies, waits for them, and re-layouts  21.3 us

profile of v1, /device:TPU:0, one launch (start us, length us, event | category | flops | bytes accessed | tf_op | source)
XLA Modules:
  0.0 184.7 jit_solution(3868022795362351207)
XLA Ops:
  0.6 1.3 reshape.7.gain_ref
  1.9 2.1 %fusion = (bf16[128,1,1024]{2,1,0:T(2,128)(2,1)S(1)}, bf16[128,1,1024]{2,1,0:T(2,128)(2,1)S(1)}) fusion(bf16[128,2,1024]{2,1,0:T(2,128)(2,1)} %param.8), kind=kLoop, calls=%fused_computation.3 | loop fusion | bytes 1048576 | tf_op jit(solution)/shard_map/slice | solution.py:251
  4.0 1.0 copy_bitcast_fusion.1
  5.0 16.4 %copy.17 = bf16[4096,2,1024]{2,0,1:T(8,128)(2,1)} copy(bf16[4096,2,1024]{2,1,0:T(2,128)(2,1)} %param.10) | data formatting | bytes 33554432 | tf_op args[4]
  21.4 158.4 %shard_map.77 = (f32[128,1024]{1,0:T(8,128)}, f32[2,128,1024]{2,1,0:T(8,128)}) custom-call(bf16[128,1024]{1,0:T(8,128)(2,1)} %q_ref.1, bf16[128,1024]{1,0:T(8,128)(2,1)} %get-tuple-element.11.k_ref, bf16[128,1024]{1,0:T(8,128)(2,1)} %get-tuple-element.10.v_ref, bf16[128,1024]{1,0:T(8,128)(2,1)} %hin_ref.1, bf16[1,4096]{1,0:T(2,128)(2,1)} %reshape.7.gain_ref, ...), custom_call_target="tpu_custom_call" | custom-call | tf_op jit(solution)/shard_map/pallas_call | solution.py:216
  179.8 3.0 %copy.11 = f32[128,2,1024]{2,1,0:T(2,128)} copy(f32[128,2,1024]{2,0,1:T(8,128)} %bitcast.9) | data formatting | bytes 2097152
  182.8 1.9 %copy.19 = f32[128,1024]{1,0:T(8,128)} copy(f32[128,1024]{1,0:T(8,128)} %get-tuple-element.14) | data formatting | bytes 1048576

commit v2 on v1

--- a/solution.py
+++ b/solution.py
@@ -31,7 +31,7 @@
 
 def fused_kernel(
     n, zn, q_ref, k_ref, v_ref, hin_ref, gain_ref, wout_ref, wkv_hbm, hid_ref, kvo_ref,
-    qkv, kv_next, w_pair, hin_all, a_send, a_all, p_send, rs, b_send, b_all, normed, kv_send, wkv,
+    qkv, kv_next, w_pair, hin_all, a_send, a_all, p_send, rs, acc, b_send, b_all, normed, kv_send, wkv,
     load_sem, local_sem, pair_send, pair_recv, in_send, in_recv, hin_send, hin_recv,
     a_ssem, a_rsem, p_ssem, p_rsem, b_ssem, b_rsem, g_ssem, g_rsem, kv_ssem, kv_rsem,
 ):
@@ -46,13 +46,20 @@
     chip_width = CORES * wout_ref.shape[1]
     pending = []
 
-    def send(src, dst, ssem, rsem, where):
-        copy = pltpu.make_async_remote_copy(
+    def remote(src, dst, ssem, rsem, where):
+        return pltpu.make_async_remote_copy(
             src_ref=src, dst_ref=dst, send_sem=ssem, recv_sem=rsem, device_id=where, device_id_type=MESH
         )
+
+    def send(*args):
+        copy = remote(*args)
         copy.start()
-        pending.append(copy)
+        pending.append((None, copy))
         return copy
+
+    def send_if(condition, copy):
+        pl.when(condition)(copy.start)
+        pending.append((condition, copy))
 
     def cols(index, size):
         return pl.ds(pl.multiple_of(index * size, size), size)
@@ -92,7 +99,6 @@
         key_ref = qkv.at[1] if it == 0 else kv_next.at[0]
         value_ref = qkv.at[2] if it == 0 else kv_next.at[1]
 
-        a_copies = []
         for i in range(groups):
             limit = (i + 1) * block
             attended = attend_block(
@@ -100,72 +106,119 @@
             )
             for side in range(CORES):
                 a_send[it, i, side] = attended[side * rows:(side + 1) * rows, :]
+        for t in range(groups):
             for d in range(1, n):
                 peer = lax.rem(c + d, n)
-                a_copies.append(send(
+                i = lax.rem(lax.div(peer, CORES) + 1 + t, groups)
+                send(
                     a_send.at[it, i, lax.rem(peer, CORES)], a_all.at[it, i, :, cols(c, HD)],
-                    a_ssem.at[it, i, d], a_rsem.at[it, i, d], {"ctx": peer},
-                ))
+                    a_ssem.at[it, t, d], a_rsem.at[it, t, d], {"ctx": peer},
+                )
+        for i in range(groups):
             a_all[it, i, :, cols(c, HD)] = a_send[it, i, core]
         if it == 0:
             own_w.wait()
             pair.wait_recv()
-        for copy in a_copies:
-            copy.wait_recv()
-
-        p_copies = []
-        for t in range(groups):
+
+        def project(t):
             i = lax.rem(k + 1 + t, groups)
             half = chip_width // CORES
+            for d in range(1, n):
+                remote(
+                    a_send.at[it, i, core], a_all.at[it, i, :, cols(c, HD)],
+                    a_ssem.at[it, t, d], a_rsem.at[it, t, d], {"ctx": lax.rem(c + d, n)},
+                ).wait_recv()
             for side in range(CORES):
                 product = jnp.dot(
                     a_all[it, i], w_pair[side], preferred_element_type=jnp.float32
                 ).astype(jnp.bfloat16)
                 for s in range(zn):
-                    p_send[it, i, s, :, side * half:(side + 1) * half] = product[s * quarter:(s + 1) * quarter, :]
-            for d in range(1, zn):
-                target = lax.rem(z + d, zn)
-                p_copies.append(send(
-                    p_send.at[it, i, target], rs.at[it, d - 1, i],
-                    p_ssem.at[it, t, d], p_rsem.at[it, t, d], {"head": target},
-                ))
-
-        b_copies = []
-        for t in range(groups):
+                    p_send[it, t, s, :, side * half:(side + 1) * half] = product[s * quarter:(s + 1) * quarter, :]
+
+        def step_copy(t, s, way):
+            return remote(
+                p_send.at[it, t, s], rs.at[it, way, t, s], p_ssem.at[it, way, t, s], p_rsem.at[it, way, t, s],
+                {"head": z + 1 if way == 0 else z - 1},
+            )
+
+        def pass_sums(t):
+            for j in range(zn - 1, 0, -1):
+                for way in range(2):
+                    s = z + j if way == 0 else z - j
+                    there = s < zn if way == 0 else s >= 0
+                    behind = z > 0 if way == 0 else z < zn - 1
+                    copy = step_copy(t, s, way)
+
+                    @pl.when(there & behind)
+                    def _():
+                        copy.wait_recv()
+                        p_send[it, t, s] = (
+                            p_send[it, t, s].astype(jnp.float32) + rs[it, way, t, s].astype(jnp.float32)
+                        ).astype(jnp.bfloat16)
+
+                    send_if(there, copy)
+
+        def finish_sums(t):
+            acc[...] = p_send[it, t, z].astype(jnp.float32)
+            for way in range(2):
+                @pl.when(z > 0 if way == 0 else z < zn - 1)
+                def _():
+                    step_copy(t, z, way).wait_recv()
+                    acc[...] += rs[it, way, t, z].astype(jnp.float32)
             i = lax.rem(k + 1 + t, groups)
-            total = p_send[it, i, z].astype(jnp.float32)
-            for d in range(1, zn):
-                p_copies[t * (zn - 1) + d - 1].wait_recv()
-                total = total + rs[it, d - 1, i].astype(jnp.float32)
-            total = total.astype(jnp.bfloat16)
             if t == groups - 1:
-                b_all[it, z, :, cols(k, chip_width)] = total
+                b_all[it, z, :, cols(k, chip_width)] = acc[...].astype(jnp.bfloat16)
             else:
-                b_send[it, t] = total
+                b_send[it, t] = acc[...].astype(jnp.bfloat16)
                 b_copies.append(send(
                     b_send.at[it, t], b_all.at[it, z, :, cols(k, chip_width)],
                     b_ssem.at[it, t], b_rsem.at[it, t], {"ctx": i * CORES + core},
                 ))
 
-        g_copies = []
-        for t in range(groups):
-            source = lax.rem(k + groups - 1 - t, groups)
+        def piece_copy(t, s, way):
+            place = b_all.at[it, s, :, cols(lax.rem(k + groups - 1 - t, groups), chip_width)]
+            return remote(
+                place, place, g_ssem.at[it, way, t, s], g_rsem.at[it, way, t, s],
+                {"head": z + 1 if way == 0 else z - 1},
+            )
+
+        def start_piece(t):
             if t < groups - 1:
                 b_copies[t].wait_recv()
-            for d in range(1, zn):
-                place = b_all.at[it, z, :, cols(source, chip_width)]
-                g_copies.append(send(
-                    place, place, g_ssem.at[it, t, d], g_rsem.at[it, t, d], {"head": lax.rem(z + d, zn)}
-                ))
+            send_if(z < zn - 1, piece_copy(t, z, 0))
+            send_if(z > 0, piece_copy(t, z, 1))
+
+        def pass_pieces(t):
+            for j in range(1, zn):
+                for way in range(2):
+                    s = z - j if way == 0 else z + j
+                    there = s >= 0 if way == 0 else s < zn
+                    ahead = z < zn - 1 if way == 0 else z > 0
+                    copy = piece_copy(t, s, way)
+
+                    @pl.when(there)
+                    def _():
+                        copy.wait_recv()
+
+                    send_if(there & ahead, copy)
+
+        b_copies = []
+        for stage in range(groups + 3):
+            if stage < groups:
+                project(stage)
+                pass_sums(stage)
+            if 0 <= stage - 1 < groups:
+                finish_sums(stage - 1)
+            if 0 <= stage - 2 < groups:
+                start_piece(stage - 2)
+            if 0 <= stage - 3 < groups:
+                pass_pieces(stage - 3)
+
         if it == 0:
             for copy in hin_copies:
                 copy.wait_recv()
-        for d in range(zn):
-            part = lax.rem(z + zn - d, zn)
-            if d > 0:
-                for t in range(groups):
-                    g_copies[t * (zn - 1) + d - 1].wait_recv()
-            span = cols(part, quarter)
+        for part in range(zn):
+            span = slice(part * quarter, (part + 1) * quarter)
             hidden = hin_all[span, :].astype(jnp.float32) + b_all[it, part].astype(jnp.float32)
             mean_square = jnp.mean(hidden * hidden, axis=1, keepdims=True)
             normed[span, :] = (
@@ -199,8 +252,11 @@
                     ))
                 kv_next[kind, cols(c, rows), :] = kv_send[kind, :, cols(c, HD)]
 
-    for copy in pending:
-        copy.wait_send()
+    for condition, copy in pending:
+        if condition is None:
+            copy.wait_send()
+        else:
+            pl.when(condition)(copy.wait_send)
 
 
 def fused_device(n, zn, hidden_in, queries, kv_prev, norm_gain, w_kv, w_out):
@@ -229,7 +285,8 @@
             pltpu.VMEM((ITERS, groups, CORES, rows, HD), bf16),
             pltpu.VMEM((ITERS, groups, rows, width), bf16),
             pltpu.VMEM((ITERS, groups, zn, quarter, chip_width), bf16),
-            pltpu.VMEM((ITERS, zn - 1, groups, quarter, chip_width), bf16),
+            pltpu.VMEM((ITERS, 2, groups, zn, quarter, chip_width), bf16),
+            pltpu.VMEM((quarter, chip_width), jnp.float32),
             pltpu.VMEM((ITERS, groups - 1, quarter, chip_width), bf16),
             pltpu.VMEM((ITERS, zn, quarter, model), bf16),
             pltpu.VMEM((rows, model), bf16),
@@ -239,9 +296,9 @@
             dma((3, n)), dma((3, n)),
             dma((zn,)), dma((zn,)),
             dma((ITERS, groups, n)), dma((ITERS, groups, n)),
-            dma((ITERS, groups, zn)), dma((ITERS, groups, zn)),
+            dma((ITERS, 2, groups, zn)), dma((ITERS, 2, groups, zn)),
             dma((ITERS, groups)), dma((ITERS, groups)),
-            dma((ITERS, groups, zn)), dma((ITERS, groups, zn)),
+            dma((ITERS, 2, groups, zn)), dma((ITERS, 2, groups, zn)),
             dma((2, n)), dma((2, n)),
         ],
         compiler_params=pltpu.CompilerParams(

time: 185 us -> 175 us (0.946)
  Pallas kernels: 158 us -> 148 us
    pallas_call x1, Pallas kernels: 158 us -> 148 us  [fused_device(): pl.pallas_call(functools.partial(fused_kernel, n, zn), out_shape=(jax.Sha...]
where the time goes in v2:
time: 175 us; the launch traced here: 174 us
  Pallas kernels  148 us (85%)
  local copies, waits for them, and re-layouts  25.7 us (15%)
    pallas_call x1, Pallas kernels, fused_device(): pl.pallas_call(functools.partial(fused_kernel, n, zn), out_shape=(jax.Sha...  148 us
    unnamed x3, local copies, waits for them, and re-layouts  21.3 us

profile of v2, /device:TPU:0, one launch (start us, length us, event | category | flops | bytes accessed | tf_op | source)
XLA Modules:
  0.0 174.1 jit_solution(5211808646728582556)
XLA Ops:
  0.6 1.3 reshape.7.gain_ref
  1.9 2.1 %fusion = (bf16[128,1,1024]{2,1,0:T(2,128)(2,1)S(1)}, bf16[128,1,1024]{2,1,0:T(2,128)(2,1)S(1)}) fusion(bf16[128,2,1024]{2,1,0:T(2,128)(2,1)} %param.8), kind=kLoop, calls=%fused_computation.3 | loop fusion | bytes 1048576 | tf_op jit(solution)/shard_map/slice | solution.py:308
  4.0 1.0 copy_bitcast_fusion.1
  5.0 16.4 %copy.17 = bf16[4096,2,1024]{2,0,1:T(8,128)(2,1)} copy(bf16[4096,2,1024]{2,1,0:T(2,128)(2,1)} %param.10) | data formatting | bytes 33554432 | tf_op args[4]
  21.4 147.8 %shard_map.77 = (f32[128,1024]{1,0:T(8,128)}, f32[2,128,1024]{2,1,0:T(8,128)}) custom-call(bf16[128,1024]{1,0:T(8,128)(2,1)} %q_ref.1, bf16[128,1024]{1,0:T(8,128)(2,1)} %get-tuple-element.11.k_ref, bf16[128,1024]{1,0:T(8,128)(2,1)} %get-tuple-element.10.v_ref, bf16[128,1024]{1,0:T(8,128)(2,1)} %hin_ref.1, bf16[1,4096]{1,0:T(2,128)(2,1)} %reshape.7.gain_ref, ...), custom_call_target="tpu_custom_call" | custom-call | tf_op jit(solution)/shard_map/pallas_call | solution.py:272
  169.2 3.0 %copy.11 = f32[128,2,1024]{2,1,0:T(2,128)} copy(f32[128,2,1024]{2,0,1:T(8,128)} %bitcast.9) | data formatting | bytes 2097152
  172.2 1.9 %copy.19 = f32[128,1024]{1,0:T(8,128)} copy(f32[128,1024]{1,0:T(8,128)} %get-tuple-element.14) | data formatting | bytes 1048576

commit v3 on v2

--- a/solution.py
+++ b/solution.py
@@ -30,8 +30,8 @@
 
 
 def fused_kernel(
-    n, zn, q_ref, k_ref, v_ref, hin_ref, gain_ref, wout_ref, wkv_hbm, hid_ref, kvo_ref,
-    qkv, kv_next, w_pair, hin_all, a_send, a_all, p_send, rs, acc, b_send, b_all, normed, kv_send, wkv,
+    n, zn, q_ref, kv_ref, hin_ref, gain_ref, wout_ref, wkv_hbm, hid_ref, kvo_ref,
+    q_all, kv_land, kv_all, w_pair, hin_all, a_send, a_all, p_send, rs, acc, b_send, b_all, scaled, squares, kv_acc, kv_send, wkv,
     load_sem, local_sem, pair_send, pair_recv, in_send, in_recv, hin_send, hin_recv,
     a_ssem, a_rsem, p_ssem, p_rsem, b_ssem, b_rsem, g_ssem, g_rsem, kv_ssem, kv_rsem,
 ):
@@ -77,14 +77,18 @@
     pl.semaphore_wait(barrier, n - 1 + zn - 1)
 
     arrivals = []
-    for kind, ref in ((1, k_ref), (0, q_ref), (2, v_ref)):
-        for d in range(1, n):
-            peer = lax.rem(c + d, n)
-            arrivals.append(send(
-                ref.at[:, cols(peer, HD)], qkv.at[kind, cols(c, rows)],
-                in_send.at[kind, d], in_recv.at[kind, d], {"ctx": peer},
-            ))
-        qkv[kind, cols(c, rows), :] = ref[:, cols(c, HD)]
+    for d in range(1, n):
+        peer = lax.rem(c + d, n)
+        arrivals.append(send(
+            kv_ref.at[:, :, cols(peer, HD)], kv_land.at[cols(c, rows)],
+            in_send.at[0, d], in_recv.at[0, d], {"ctx": peer},
+        ))
+        arrivals.append(send(
+            q_ref.at[:, cols(peer, HD)], q_all.at[cols(c, rows)],
+            in_send.at[1, d], in_recv.at[1, d], {"ctx": peer},
+        ))
+    kv_land[cols(c, rows), :, :] = kv_ref[:, :, cols(c, HD)]
+    q_all[cols(c, rows), :] = q_ref[:, cols(c, HD)]
     pair = send(wout_ref, w_pair.at[core], pair_send, pair_recv, {"ctx": k * CORES + 1 - core})
     hin_copies = [
         send(hin_ref, hin_all.at[:, cols(z, width)], hin_send.at[d], hin_recv.at[d],
@@ -96,13 +100,14 @@
     for it in range(ITERS):
         for copy in arrivals:
             copy.wait_recv()
-        key_ref = qkv.at[1] if it == 0 else kv_next.at[0]
-        value_ref = qkv.at[2] if it == 0 else kv_next.at[1]
+        if it == 0:
+            for kind in range(2):
+                kv_all[it, kind] = kv_land[:, kind, :]
 
         for i in range(groups):
             limit = (i + 1) * block
             attended = attend_block(
-                qkv[0, i * block:limit, :], key_ref[0:limit, :], value_ref[0:limit, :], i * block
+                q_all[i * block:limit, :], kv_all[it, 0, 0:limit, :], kv_all[it, 1, 0:limit, :], i * block
             )
             for side in range(CORES):
                 a_send[it, i, side] = attended[side * rows:(side + 1) * rows, :]
@@ -202,6 +207,41 @@
 
                     send_if(there & ahead, copy)
 
+        def consume(t):
+            place = cols(lax.rem(k + groups - 1 - t, groups), chip_width)
+            hidden = hin_all[:, place].astype(jnp.float32) + b_all[it, :, :, place].astype(
+                jnp.float32
+            ).reshape(rows, chip_width)
+            square = jnp.sum(hidden * hidden, axis=1, keepdims=True)
+            scaled[...] = (hidden * gain_ref[:, place].astype(jnp.float32)).astype(jnp.bfloat16)
+            squares[...] = square if t == 0 else squares[...] + square
+            scale = lax.rsqrt(squares[...] / hin_all.shape[1] + EPSILON)
+            copies = []
+            for kind in range(2):
+                @pl.loop(0, width // 256)
+                def _(j):
+                    product = jnp.dot(
+                        scaled[...], wkv[kind, place, cols(j, 256)], preferred_element_type=jnp.float32
+                    )
+                    if t > 0:
+                        product = product + kv_acc[kind, :, cols(j, 256)]
+                    if t < groups - 1:
+                        kv_acc[kind, :, cols(j, 256)] = product
+                    elif it == ITERS - 1:
+                        kvo_ref[:, kind, cols(j, 256)] = product * scale
+                    else:
+                        kv_send[kind, :, cols(j, 256)] = (product * scale).astype(jnp.bfloat16)
+
+                if t == groups - 1 and it < ITERS - 1:
+                    for d in range(1, n):
+                        peer = lax.rem(c + d, n)
+                        copies.append(send(
+                            kv_send.at[kind, :, cols(peer, HD)], kv_all.at[it + 1, kind, cols(c, rows)],
+                            kv_ssem.at[kind, d], kv_rsem.at[kind, d], {"ctx": peer},
+                        ))
+                    kv_all[it + 1, kind, cols(c, rows), :] = kv_send[kind, :, cols(c, HD)]
+            return copies
+
         b_copies = []
         for stage in range(groups + 3):
             if stage < groups:
@@ -211,46 +251,21 @@
                 finish_sums(stage - 1)
             if 0 <= stage - 2 < groups:
                 start_piece(stage - 2)
+            if it == 0 and stage == 4:
+                for copy in hin_copies:
+                    copy.wait_recv()
+                load.wait()
+            if stage - 4 == groups - 2:
+                consume(stage - 4)
             if 0 <= stage - 3 < groups:
                 pass_pieces(stage - 3)
-
-        if it == 0:
-            for copy in hin_copies:
-                copy.wait_recv()
-        for part in range(zn):
-            span = slice(part * quarter, (part + 1) * quarter)
-            hidden = hin_all[span, :].astype(jnp.float32) + b_all[it, part].astype(jnp.float32)
-            mean_square = jnp.mean(hidden * hidden, axis=1, keepdims=True)
-            normed[span, :] = (
-                hidden * lax.rsqrt(mean_square + EPSILON) * gain_ref[...].astype(jnp.float32)
-            ).astype(jnp.bfloat16)
-            if it == ITERS - 1:
-                hid_ref[span, :] = hin_ref[span, :].astype(jnp.float32) + b_all[
-                    it, part, :, cols(z, width)
-                ].astype(jnp.float32)
-
-        if it == 0:
-            load.wait()
-        arrivals = []
-        for kind in range(2):
-            @pl.loop(0, width // 256)
-            def _(j):
-                product = jnp.dot(
-                    normed[...], wkv[kind, :, cols(j, 256)], preferred_element_type=jnp.float32
-                )
-                if it == ITERS - 1:
-                    kvo_ref[kind, :, cols(j, 256)] = product
-                else:
-                    kv_send[kind, :, cols(j, 256)] = product.astype(jnp.bfloat16)
-
-            if it < ITERS - 1:
-                for d in range(1, n):
-                    peer = lax.rem(c + d, n)
-                    arrivals.append(send(
-                        kv_send.at[kind, :, cols(peer, HD)], kv_next.at[kind, cols(c, rows)],
-                        kv_ssem.at[kind, d], kv_rsem.at[kind, d], {"ctx": peer},
-                    ))
-                kv_next[kind, cols(c, rows), :] = kv_send[kind, :, cols(c, HD)]
+            if 0 <= stage - 4 < groups - 2:
+                consume(stage - 4)
+        arrivals = consume(groups - 1)
+        if it == ITERS - 1:
+            hid_ref[...] = hin_ref[...].astype(jnp.float32) + b_all[it, :, :, cols(z, width)].astype(
+                jnp.float32
+            ).reshape(rows, width)
 
     for condition, copy in pending:
         if condition is None:
@@ -269,17 +284,18 @@
     vmem = pl.BlockSpec(memory_space=pltpu.VMEM)
     bf16 = jnp.bfloat16
     dma = pltpu.SemaphoreType.DMA
-    hidden_out, kv = pl.pallas_call(
+    return pl.pallas_call(
         functools.partial(fused_kernel, n, zn),
         out_shape=(
             jax.ShapeDtypeStruct((rows, width), jnp.float32),
-            jax.ShapeDtypeStruct((2, rows, width), jnp.float32),
+            jax.ShapeDtypeStruct((rows, 2, width), jnp.float32),
         ),
-        in_specs=[vmem] * 6 + [pl.BlockSpec(memory_space=pl.ANY)],
+        in_specs=[vmem] * 5 + [pl.BlockSpec(memory_space=pl.ANY)],
         out_specs=(vmem, vmem),
         scratch_shapes=[
-            pltpu.VMEM((3, tokens, HD), bf16),
-            pltpu.VMEM((2, tokens, HD), bf16),
+            pltpu.VMEM((tokens, HD), bf16),
+            pltpu.VMEM((tokens, 2, HD), bf16),
+            pltpu.VMEM((ITERS, 2, tokens, HD), bf16),
             pltpu.VMEM((CORES,) + w_out.shape, bf16),
             pltpu.VMEM((rows, model), bf16),
             pltpu.VMEM((ITERS, groups, CORES, rows, HD), bf16),
@@ -289,11 +305,13 @@
             pltpu.VMEM((quarter, chip_width), jnp.float32),
             pltpu.VMEM((ITERS, groups - 1, quarter, chip_width), bf16),
             pltpu.VMEM((ITERS, zn, quarter, model), bf16),
-            pltpu.VMEM((rows, model), bf16),
+            pltpu.VMEM((rows, chip_width), bf16),
+            pltpu.VMEM((rows, 1), jnp.float32),
+            pltpu.VMEM((2, rows, width), jnp.float32),
             pltpu.VMEM((2, rows, width), bf16),
             pltpu.VMEM((2, model, width), bf16),
             dma, dma, dma, dma,
-            dma((3, n)), dma((3, n)),
+            dma((2, n)), dma((2, n)),
             dma((zn,)), dma((zn,)),
             dma((ITERS, groups, n)), dma((ITERS, groups, n)),
             dma((ITERS, 2, groups, zn)), dma((ITERS, 2, groups, zn)),
@@ -302,13 +320,9 @@
             dma((2, n)), dma((2, n)),
         ],
         compiler_params=pltpu.CompilerParams(
-            collective_id=0, has_side_effects=True, vmem_limit_bytes=56 * 1024 * 1024
+            collective_id=0, has_side_effects=True, vmem_limit_bytes=58 * 1024 * 1024
         ),
-    )(
-        queries, kv_prev[:, 0], kv_prev[:, 1], hidden_in, norm_gain.reshape(1, model), w_out,
-        w_kv.transpose(1, 0, 2),
-    )
-    return hidden_out, kv.transpose(1, 0, 2)
+    )(queries, kv_prev, hidden_in, norm_gain.reshape(1, model), w_out, w_kv.transpose(1, 0, 2))
 
 
 def attend_gathered(query_heads, key_value, row_start):

time: 175 us -> 173 us (0.989)
  local copies, waits for them, and re-layouts: 25.7 us -> 21.9 us
  Pallas kernels: 148 us -> 150 us
    pallas_call x1, Pallas kernels: 148 us -> 150 us  [fused_device(): pl.pallas_call(functools.partial(fused_kernel, n, zn), out_shape=(jax.Sha...]
    slice x1 -> x0, local copies, waits for them, and re-layouts: 2.1 us -> none  [fused_device(): kv_prev[:, 1]]
where the time goes in v3:
time: 173 us
  Pallas kernels  150 us (87%)
  local copies, waits for them, and re-layouts  21.9 us (13%)
    pallas_call x1, Pallas kernels, fused_device(): pl.pallas_call(functools.partial(fused_kernel, n, zn), out_shape=(jax.Sha...  150 us
    unnamed x3, local copies, waits for them, and re-layouts  20.6 us

profile of v3, /device:TPU:0, one launch (start us, length us, event | category | flops | bytes accessed | tf_op | source)
XLA Modules:
  0.0 172.8 jit_solution(16996982612549858914)
XLA Ops:
  0.6 1.3 reshape.7.gain_ref
  1.9 16.4 %copy.10 = bf16[4096,2,1024]{2,0,1:T(8,128)(2,1)} copy(bf16[4096,2,1024]{2,1,0:T(2,128)(2,1)} %param.10) | data formatting | bytes 33554432 | tf_op args[4]
  18.4 150.3 %shard_map.77 = (f32[128,1024]{1,0:T(8,128)}, f32[128,2,1024]{2,1,0:T(2,128)}) custom-call(bf16[128,1024]{1,0:T(8,128)(2,1)} %q_ref.1, bf16[128,2,1024]{2,1,0:T(2,128)(2,1)} %kv_ref.1, bf16[128,1024]{1,0:T(8,128)(2,1)} %hin_ref.1, bf16[1,4096]{1,0:T(2,128)(2,1)} %reshape.7.gain_ref, bf16[1024,512]{1,0:T(8,128)(2,1)} %wout_ref.1, bf16[2,4096,1024]{2,1,0:T(8,128)(2,1)} %bitcast.3), custom_call_target="tpu_custom_call" | custom-call | tf_op jit(solution)/shard_map/pallas_call | solution.py:287
  168.7 1.9 %copy.13 = f32[128,1024]{1,0:T(8,128)} copy(f32[128,1024]{1,0:T(8,128)} %get-tuple-element.4) | data formatting | bytes 1048576
  170.5 2.3 %copy.14 = f32[128,2,1024]{2,1,0:T(2,128)} copy(f32[128,2,1024]{2,1,0:T(2,128)} %get-tuple-element.5) | data formatting | bytes 2097152

commit v4 on v3

--- a/solution.py
+++ b/solution.py
@@ -146,22 +146,23 @@
                 {"head": z + 1 if way == 0 else z - 1},
             )
 
-        def pass_sums(t):
-            for j in range(zn - 1, 0, -1):
-                for way in range(2):
-                    s = z + j if way == 0 else z - j
-                    there = s < zn if way == 0 else s >= 0
-                    behind = z > 0 if way == 0 else z < zn - 1
-                    copy = step_copy(t, s, way)
-
-                    @pl.when(there & behind)
-                    def _():
-                        copy.wait_recv()
-                        p_send[it, t, s] = (
-                            p_send[it, t, s].astype(jnp.float32) + rs[it, way, t, s].astype(jnp.float32)
-                        ).astype(jnp.bfloat16)
-
-                    send_if(there, copy)
+        def pass_sums(t, hop):
+            for way in range(2):
+                @pl.when(z == (hop if way == 0 else zn - 1 - hop))
+                def _():
+                    for j in range(zn - 1 - hop, 0, -1):
+                        s = hop + j if way == 0 else zn - 1 - hop - j
+                        copy = step_copy(t, s, way)
+                        if hop > 0:
+                            copy.wait_recv()
+                            p_send[it, t, s] = (
+                                p_send[it, t, s].astype(jnp.float32) + rs[it, way, t, s].astype(jnp.float32)
+                            ).astype(jnp.bfloat16)
+                        copy.start()
+
+                for j in range(zn - 1 - hop, 0, -1):
+                    s = hop + j if way == 0 else zn - 1 - hop - j
+                    pending.append((z == (hop if way == 0 else zn - 1 - hop), step_copy(t, s, way)))
 
         def finish_sums(t):
             acc[...] = p_send[it, t, z].astype(jnp.float32)
@@ -193,19 +194,14 @@
             send_if(z < zn - 1, piece_copy(t, z, 0))
             send_if(z > 0, piece_copy(t, z, 1))
 
-        def pass_pieces(t):
-            for j in range(1, zn):
-                for way in range(2):
-                    s = z - j if way == 0 else z + j
-                    there = s >= 0 if way == 0 else s < zn
-                    ahead = z < zn - 1 if way == 0 else z > 0
-                    copy = piece_copy(t, s, way)
-
-                    @pl.when(there)
-                    def _():
-                        copy.wait_recv()
-
-                    send_if(there & ahead, copy)
+        def pass_pieces(t, j):
+            for way in range(2):
+                s = z - j if way == 0 else z + j
+                there = s >= 0 if way == 0 else s < zn
+                ahead = z < zn - 1 if way == 0 else z > 0
+                copy = piece_copy(t, s, way)
+                pl.when(there)(copy.wait_recv)
+                send_if(there & ahead, copy)
 
         def consume(t):
             place = cols(lax.rem(k + groups - 1 - t, groups), chip_width)
@@ -243,24 +239,21 @@
             return copies
 
         b_copies = []
-        for stage in range(groups + 3):
-            if stage < groups:
-                project(stage)
-                pass_sums(stage)
-            if 0 <= stage - 1 < groups:
-                finish_sums(stage - 1)
-            if 0 <= stage - 2 < groups:
-                start_piece(stage - 2)
-            if it == 0 and stage == 4:
+        tasks = [project]
+        tasks += [functools.partial(pass_sums, hop=hop) for hop in range(zn - 1)]
+        tasks += [finish_sums, start_piece]
+        tasks += [functools.partial(pass_pieces, j=j) for j in range(1, zn)]
+        lags = [0] + list(range(zn - 1)) + list(range(zn - 1, 2 * zn))
+        for stage in range(groups + 2 * zn):
+            for task, lag in zip(tasks, lags):
+                if 0 <= stage - lag < groups:
+                    task(stage - lag)
+            if stage == 2 * zn and it == 0:
                 for copy in hin_copies:
                     copy.wait_recv()
                 load.wait()
-            if stage - 4 == groups - 2:
-                consume(stage - 4)
-            if 0 <= stage - 3 < groups:
-                pass_pieces(stage - 3)
-            if 0 <= stage - 4 < groups - 2:
-                consume(stage - 4)
+            if 0 <= stage - 2 * zn < groups - 1:
+                consume(stage - 2 * zn)
         arrivals = consume(groups - 1)
         if it == ITERS - 1:
             hid_ref[...] = hin_ref[...].astype(jnp.float32) + b_all[it, :, :, cols(z, width)].astype(

time: 173 us -> 158 us (0.913)
  Pallas kernels: 150 us -> 135 us
    pallas_call x1, Pallas kernels: 150 us -> 135 us  [fused_device(): pl.pallas_call(functools.partial(fused_kernel, n, zn), out_shape=(jax.Sha...]
where the time goes in v4:
time: 158 us
  Pallas kernels  135 us (85%)
  local copies, waits for them, and re-layouts  21.9 us (14%)
    pallas_call x1, Pallas kernels, fused_device(): pl.pallas_call(functools.partial(fused_kernel, n, zn), out_shape=(jax.Sha...  135 us
    unnamed x3, local copies, waits for them, and re-layouts  20.6 us

profile of v4, /device:TPU:0, one launch (start us, length us, event | category | flops | bytes accessed | tf_op | source)
XLA Modules:
  0.0 157.6 jit_solution(7962512970698130819)
XLA Ops:
  0.6 1.3 reshape.7.gain_ref
  1.9 16.4 %copy.10 = bf16[4096,2,1024]{2,0,1:T(8,128)(2,1)} copy(bf16[4096,2,1024]{2,1,0:T(2,128)(2,1)} %param.10) | data formatting | bytes 33554432 | tf_op args[4]
  18.4 135.0 %shard_map.77 = (f32[128,1024]{1,0:T(8,128)}, f32[128,2,1024]{2,1,0:T(2,128)}) custom-call(bf16[128,1024]{1,0:T(8,128)(2,1)} %q_ref.1, bf16[128,2,1024]{2,1,0:T(2,128)(2,1)} %kv_ref.1, bf16[128,1024]{1,0:T(8,128)(2,1)} %hin_ref.1, bf16[1,4096]{1,0:T(2,128)(2,1)} %reshape.7.gain_ref, bf16[1024,512]{1,0:T(8,128)(2,1)} %wout_ref.1, bf16[2,4096,1024]{2,1,0:T(8,128)(2,1)} %bitcast.3), custom_call_target="tpu_custom_call" | custom-call | tf_op jit(solution)/shard_map/pallas_call | solution.py:280
  153.4 1.9 %copy.13 = f32[128,1024]{1,0:T(8,128)} copy(f32[128,1024]{1,0:T(8,128)} %get-tuple-element.4) | data formatting | bytes 1048576
  155.3 2.3 %copy.14 = f32[128,2,1024]{2,1,0:T(2,128)} copy(f32[128,2,1024]{2,1,0:T(2,128)} %get-tuple-element.5) | data formatting | bytes 2097152

commit v5 on v4

--- a/solution.py
+++ b/solution.py
@@ -31,9 +31,9 @@
 
 def fused_kernel(
     n, zn, q_ref, kv_ref, hin_ref, gain_ref, wout_ref, wkv_hbm, hid_ref, kvo_ref,
-    q_all, kv_land, kv_all, w_pair, hin_all, a_send, a_all, p_send, rs, acc, b_send, b_all, scaled, squares, kv_acc, kv_send, wkv,
+    q_all, kv_land, kv_all, w_pair, hin_all, a_send, a_all, p_send, rs, acc, b_send, b_all, scaled, squares, kv_acc, kv_send, kv_back, wkv, staged,
     load_sem, local_sem, pair_send, pair_recv, in_send, in_recv, hin_send, hin_recv,
-    a_ssem, a_rsem, p_ssem, p_rsem, b_ssem, b_rsem, g_ssem, g_rsem, kv_ssem, kv_rsem,
+    a_ssem, a_rsem, p_ssem, p_rsem, b_ssem, b_rsem, g_ssem, g_rsem, kv_ssem, kv_rsem, x_ssem, x_rsem, y_ssem, y_rsem,
 ):
     c = lax.axis_index("ctx")
     z = lax.axis_index("head")
@@ -64,8 +64,29 @@
     def cols(index, size):
         return pl.ds(pl.multiple_of(index * size, size), size)
 
-    load = pltpu.make_async_copy(wkv_hbm, wkv, load_sem)
-    load.start()
+    chunk = staged.shape[1]
+    chunk_count = wkv_hbm.shape[0] // chunk
+    sibling = {"ctx": k * CORES + 1 - core}
+
+    def load(j):
+        slot = lax.rem(j, 2)
+        return pltpu.make_async_copy(wkv_hbm.at[cols(j, chunk)], staged.at[slot], load_sem.at[slot])
+
+    def part_weights(first, last):
+        @pl.loop(first, last)
+        def _(j):
+            load(j).wait()
+            for kind in range(CORES):
+                @pl.when(core == kind)
+                def _():
+                    wkv[cols(j, chunk), :] = staged[lax.rem(j, 2), :, kind, :]
+
+            @pl.when(j + 2 < chunk_count)
+            def _():
+                load(j + 2).start()
+
+    load(jnp.int32(0)).start()
+    load(jnp.int32(1)).start()
     own_w = pltpu.make_async_copy(wout_ref, w_pair.at[core], local_sem)
     own_w.start()
 
@@ -79,27 +100,32 @@
     arrivals = []
     for d in range(1, n):
         peer = lax.rem(c + d, n)
-        arrivals.append(send(
+        arrivals.append((None, send(
             kv_ref.at[:, :, cols(peer, HD)], kv_land.at[cols(c, rows)],
             in_send.at[0, d], in_recv.at[0, d], {"ctx": peer},
-        ))
-        arrivals.append(send(
+        )))
+        arrivals.append((None, send(
             q_ref.at[:, cols(peer, HD)], q_all.at[cols(c, rows)],
             in_send.at[1, d], in_recv.at[1, d], {"ctx": peer},
-        ))
+        )))
     kv_land[cols(c, rows), :, :] = kv_ref[:, :, cols(c, HD)]
     q_all[cols(c, rows), :] = q_ref[:, cols(c, HD)]
-    pair = send(wout_ref, w_pair.at[core], pair_send, pair_recv, {"ctx": k * CORES + 1 - core})
+    pair = send(wout_ref, w_pair.at[core], pair_send, pair_recv, sibling)
     hin_copies = [
-        send(hin_ref, hin_all.at[:, cols(z, width)], hin_send.at[d], hin_recv.at[d],
+        send(hin_ref, hin_all.at[core, :, cols(z, width)], hin_send.at[d], hin_recv.at[d],
              {"head": lax.rem(z + d, zn)})
         for d in range(1, zn)
     ]
-    hin_all[:, cols(z, width)] = hin_ref[...]
-
+    hin_all[core, :, cols(z, width)] = hin_ref[...]
+
+    plan = [chunk_count * part // 16 for part in (0, 6, 11, 12, 13, 14, 16)]
+    part_weights(plan[0], plan[1])
     for it in range(ITERS):
-        for copy in arrivals:
-            copy.wait_recv()
+        for condition, copy in arrivals:
+            if condition is None:
+                copy.wait_recv()
+            else:
+                pl.when(condition)(copy.wait_recv)
         if it == 0:
             for kind in range(2):
                 kv_all[it, kind] = kv_land[:, kind, :]
@@ -122,6 +148,7 @@
         for i in range(groups):
             a_all[it, i, :, cols(c, HD)] = a_send[it, i, core]
         if it == 0:
+            part_weights(plan[1], plan[2])
             own_w.wait()
             pair.wait_recv()
 
@@ -173,24 +200,29 @@
                     acc[...] += rs[it, way, t, z].astype(jnp.float32)
             i = lax.rem(k + 1 + t, groups)
             if t == groups - 1:
-                b_all[it, z, :, cols(k, chip_width)] = acc[...].astype(jnp.bfloat16)
+                b_all[it, core, z, :, cols(k, chip_width)] = acc[...].astype(jnp.bfloat16)
             else:
                 b_send[it, t] = acc[...].astype(jnp.bfloat16)
                 b_copies.append(send(
-                    b_send.at[it, t], b_all.at[it, z, :, cols(k, chip_width)],
+                    b_send.at[it, t], b_all.at[it, core, z, :, cols(k, chip_width)],
                     b_ssem.at[it, t], b_rsem.at[it, t], {"ctx": i * CORES + core},
                 ))
 
         def piece_copy(t, s, way):
-            place = b_all.at[it, s, :, cols(lax.rem(k + groups - 1 - t, groups), chip_width)]
+            place = b_all.at[it, core, s, :, cols(lax.rem(k + groups - 1 - t, groups), chip_width)]
             return remote(
                 place, place, g_ssem.at[it, way, t, s], g_rsem.at[it, way, t, s],
                 {"head": z + 1 if way == 0 else z - 1},
             )
 
+        def pair_copy(t, s, side):
+            place = b_all.at[it, side, s, :, cols(lax.rem(k + groups - 1 - t, groups), chip_width)]
+            return remote(place, place, x_ssem.at[it, t, s], x_rsem.at[it, t, s], sibling)
+
         def start_piece(t):
             if t < groups - 1:
                 b_copies[t].wait_recv()
+            send_if(z >= 0, pair_copy(t, z, core))
             send_if(z < zn - 1, piece_copy(t, z, 0))
             send_if(z > 0, piece_copy(t, z, 1))
 
@@ -202,41 +234,64 @@
                 copy = piece_copy(t, s, way)
                 pl.when(there)(copy.wait_recv)
                 send_if(there & ahead, copy)
+                send_if(there, pair_copy(t, s, core))
 
         def consume(t):
             place = cols(lax.rem(k + groups - 1 - t, groups), chip_width)
-            hidden = hin_all[:, place].astype(jnp.float32) + b_all[it, :, :, place].astype(
-                jnp.float32
-            ).reshape(rows, chip_width)
+            for part in range(zn):
+                pair_copy(t, part, 1 - core).wait_recv()
+            both = CORES * rows
+            hidden = hin_all[:, :, place].astype(jnp.float32).reshape(both, chip_width) + b_all[
+                it, :, :, :, place
+            ].astype(jnp.float32).reshape(both, chip_width)
             square = jnp.sum(hidden * hidden, axis=1, keepdims=True)
             scaled[...] = (hidden * gain_ref[:, place].astype(jnp.float32)).astype(jnp.bfloat16)
             squares[...] = square if t == 0 else squares[...] + square
-            scale = lax.rsqrt(squares[...] / hin_all.shape[1] + EPSILON)
-            copies = []
-            for kind in range(2):
-                @pl.loop(0, width // 256)
-                def _(j):
-                    product = jnp.dot(
-                        scaled[...], wkv[kind, place, cols(j, 256)], preferred_element_type=jnp.float32
+            scale = lax.rsqrt(squares[...] / hin_all.shape[2] + EPSILON)
+
+            @pl.loop(0, width // 256)
+            def _(j):
+                product = jnp.dot(
+                    scaled[...], wkv[place, cols(j, 256)], preferred_element_type=jnp.float32
+                )
+                if t > 0:
+                    product = product + kv_acc[:, cols(j, 256)]
+                if t == groups - 1:
+                    product = product * scale
+                if t == groups - 1 and it < ITERS - 1:
+                    kv_send[:, cols(j, 256)] = product.astype(jnp.bfloat16)
+                else:
+                    kv_acc[:, cols(j, 256)] = product
+
+            if t < groups - 1:
+                return []
+            if it < ITERS - 1:
+                copies = []
+                for d in range(1, n):
+                    peer = lax.rem(c + d, n)
+                    send(
+                        kv_send.at[:, cols(peer, HD)], kv_all.at[it + 1, core, cols(k, both)],
+                        kv_ssem.at[d], kv_rsem.at[core, k], {"ctx": peer},
                     )
-                    if t > 0:
-                        product = product + kv_acc[kind, :, cols(j, 256)]
-                    if t < groups - 1:
-                        kv_acc[kind, :, cols(j, 256)] = product
-                    elif it == ITERS - 1:
-                        kvo_ref[:, kind, cols(j, 256)] = product * scale
-                    else:
-                        kv_send[kind, :, cols(j, 256)] = (product * scale).astype(jnp.bfloat16)
-
-                if t == groups - 1 and it < ITERS - 1:
-                    for d in range(1, n):
-                        peer = lax.rem(c + d, n)
-                        copies.append(send(
-                            kv_send.at[kind, :, cols(peer, HD)], kv_all.at[it + 1, kind, cols(c, rows)],
-                            kv_ssem.at[kind, d], kv_rsem.at[kind, d], {"ctx": peer},
-                        ))
-                    kv_all[it + 1, kind, cols(c, rows), :] = kv_send[kind, :, cols(c, HD)]
-            return copies
+                kv_all[it + 1, core, cols(k, both), :] = kv_send[:, cols(c, HD)]
+                for kind in range(CORES):
+                    for chip in range(groups):
+                        copies.append(((core != kind) | (k != chip), remote(
+                            kv_send.at[:, cols(c, HD)], kv_all.at[it + 1, kind, cols(chip, both)],
+                            kv_ssem.at[0], kv_rsem.at[kind, chip], sibling,
+                        )))
+                return copies
+            back = send(kv_acc.at[cols(1 - core, rows)], kv_back, y_ssem, y_rsem, sibling)
+            for kind in range(CORES):
+                @pl.when(core == kind)
+                def _():
+                    kvo_ref[:, kind, :] = kv_acc[kind * rows:(kind + 1) * rows, :]
+            back.wait_recv()
+            for kind in range(CORES):
+                @pl.when(core == kind)
+                def _():
+                    kvo_ref[:, 1 - kind, :] = kv_back[...]
+            return []
 
         b_copies = []
         tasks = [project]
@@ -248,15 +303,19 @@
             for task, lag in zip(tasks, lags):
                 if 0 <= stage - lag < groups:
                     task(stage - lag)
-            if stage == 2 * zn and it == 0:
+            if it == 0 and stage < groups:
+                part_weights(plan[2 + stage], plan[3 + stage])
+            if it == 0 and stage == groups:
                 for copy in hin_copies:
                     copy.wait_recv()
-                load.wait()
+                hin_pair = send(hin_all.at[core], hin_all.at[core], hin_send.at[0], hin_recv.at[0], sibling)
+            if it == 0 and stage == 2 * zn:
+                hin_pair.wait_recv()
             if 0 <= stage - 2 * zn < groups - 1:
                 consume(stage - 2 * zn)
         arrivals = consume(groups - 1)
         if it == ITERS - 1:
-            hid_ref[...] = hin_ref[...].astype(jnp.float32) + b_all[it, :, :, cols(z, width)].astype(
+            hid_ref[...] = hin_ref[...].astype(jnp.float32) + b_all[it, core, :, :, cols(z, width)].astype(
                 jnp.float32
             ).reshape(rows, width)
 
@@ -290,32 +349,36 @@
             pltpu.VMEM((tokens, 2, HD), bf16),
             pltpu.VMEM((ITERS, 2, tokens, HD), bf16),
             pltpu.VMEM((CORES,) + w_out.shape, bf16),
-            pltpu.VMEM((rows, model), bf16),
+            pltpu.VMEM((CORES, rows, model), bf16),
             pltpu.VMEM((ITERS, groups, CORES, rows, HD), bf16),
             pltpu.VMEM((ITERS, groups, rows, width), bf16),
             pltpu.VMEM((ITERS, groups, zn, quarter, chip_width), bf16),
             pltpu.VMEM((ITERS, 2, groups, zn, quarter, chip_width), bf16),
             pltpu.VMEM((quarter, chip_width), jnp.float32),
             pltpu.VMEM((ITERS, groups - 1, quarter, chip_width), bf16),
-            pltpu.VMEM((ITERS, zn, quarter, model), bf16),
-            pltpu.VMEM((rows, chip_width), bf16),
-            pltpu.VMEM((rows, 1), jnp.float32),
-            pltpu.VMEM((2, rows, width), jnp.float32),
-            pltpu.VMEM((2, rows, width), bf16),
-            pltpu.VMEM((2, model, width), bf16),
-            dma, dma, dma, dma,
+            pltpu.VMEM((ITERS, CORES, zn, quarter, model), bf16),
+            pltpu.VMEM((CORES * rows, chip_width), bf16),
+            pltpu.VMEM((CORES * rows, 1), jnp.float32),
+            pltpu.VMEM((CORES * rows, width), jnp.float32),
+            pltpu.VMEM((CORES * rows, width), bf16),
+            pltpu.VMEM((rows, width), jnp.float32),
+            pltpu.VMEM((model, width), bf16),
+            pltpu.VMEM((2, 64, 2, width), bf16),
+            dma((2,)), dma, dma, dma,
             dma((2, n)), dma((2, n)),
             dma((zn,)), dma((zn,)),
             dma((ITERS, groups, n)), dma((ITERS, groups, n)),
             dma((ITERS, 2, groups, zn)), dma((ITERS, 2, groups, zn)),
             dma((ITERS, groups)), dma((ITERS, groups)),
             dma((ITERS, 2, groups, zn)), dma((ITERS, 2, groups, zn)),
-            dma((2, n)), dma((2, n)),
+            dma((n,)), dma((CORES, groups)),
+            dma((ITERS, groups, zn)), dma((ITERS, groups, zn)),
+            dma, dma,
         ],
         compiler_params=pltpu.CompilerParams(
             collective_id=0, has_side_effects=True, vmem_limit_bytes=58 * 1024 * 1024
         ),
-    )(queries, kv_prev, hidden_in, norm_gain.reshape(1, model), w_out, w_kv.transpose(1, 0, 2))
+    )(queries, kv_prev, hidden_in, norm_gain.reshape(1, model), w_out, w_kv)
 
 
 def attend_gathered(query_heads, key_value, row_start):

time: 158 us -> 154 us (0.975)
  local copies, waits for them, and re-layouts: 21.9 us -> 5.46 us
  Pallas kernels: 135 us -> 146 us
    unnamed x3 -> x2, local copies, waits for them, and re-layouts: 20.6 us -> 4.15 us
    pallas_call x1, Pallas kernels: 135 us -> 146 us  [fused_device(): pl.pallas_call(functools.partial(fused_kernel, n, zn), out_shape=(jax.Sha...]
where the time goes in v5:
time: 154 us; the launch traced here: 153 us
  Pallas kernels  146 us (95%)
  local copies, waits for them, and re-layouts  5.46 us (4%)
    pallas_call x1, Pallas kernels, fused_device(): pl.pallas_call(functools.partial(fused_kernel, n, zn), out_shape=(jax.Sha...  146 us
    unnamed x2, local copies, waits for them, and re-layouts  4.15 us

profile of v5, /device:TPU:0, one launch (start us, length us, event | category | flops | bytes accessed | tf_op | source)
XLA Modules:
  0.0 152.6 jit_solution(14989688754454480207)
XLA Ops:
  0.6 1.3 reshape.7.gain_ref
  1.9 146.5 %shard_map.77 = (f32[128,1024]{1,0:T(8,128)}, f32[128,2,1024]{2,1,0:T(2,128)}) custom-call(bf16[128,1024]{1,0:T(8,128)(2,1)} %q_ref.1, bf16[128,2,1024]{2,1,0:T(2,128)(2,1)} %kv_ref.1, bf16[128,1024]{1,0:T(8,128)(2,1)} %hin_ref.1, bf16[1,4096]{1,0:T(2,128)(2,1)} %reshape.7.gain_ref, bf16[1024,512]{1,0:T(8,128)(2,1)} %wout_ref.1, bf16[4096,2,1024]{2,1,0:T(2,128)(2,1)} %wkv_hbm.1), custom_call_target="tpu_custom_call" | custom-call | tf_op jit(solution)/shard_map/pallas_call | solution.py:339
  148.4 1.9 %copy.10 = f32[128,1024]{1,0:T(8,128)} copy(f32[128,1024]{1,0:T(8,128)} %get-tuple-element.4) | data formatting | bytes 1048576
  150.3 2.3 %copy.11 = f32[128,2,1024]{2,1,0:T(2,128)} copy(f32[128,2,1024]{2,1,0:T(2,128)} %get-tuple-element.5) | data formatting | bytes 2097152

commit v6 on v5

--- a/solution.py
+++ b/solution.py
@@ -68,9 +68,14 @@
     chunk_count = wkv_hbm.shape[0] // chunk
     sibling = {"ctx": k * CORES + 1 - core}
 
+    def span_of(j):
+        each = chip_width // chunk
+        first = lax.rem(k + groups - 1 - lax.div(j, each), groups)
+        return cols(lax.rem(first + groups, groups) * each + lax.rem(j, each), chunk)
+
     def load(j):
         slot = lax.rem(j, 2)
-        return pltpu.make_async_copy(wkv_hbm.at[cols(j, chunk)], staged.at[slot], load_sem.at[slot])
+        return pltpu.make_async_copy(wkv_hbm.at[span_of(j)], staged.at[slot], load_sem.at[slot])
 
     def part_weights(first, last):
         @pl.loop(first, last)
@@ -79,7 +84,7 @@
             for kind in range(CORES):
                 @pl.when(core == kind)
                 def _():
-                    wkv[cols(j, chunk), :] = staged[lax.rem(j, 2), :, kind, :]
+                    wkv[span_of(j), :] = staged[lax.rem(j, 2), :, kind, :]
 
             @pl.when(j + 2 < chunk_count)
             def _():
@@ -118,7 +123,7 @@
     ]
     hin_all[core, :, cols(z, width)] = hin_ref[...]
 
-    plan = [chunk_count * part // 16 for part in (0, 6, 11, 12, 13, 14, 16)]
+    plan = [chunk_count * part // 64 for part in (0, 12, 16, 18, 20, 22, 24, 28, 32, 36, 40, 46, 54, 64)]
     part_weights(plan[0], plan[1])
     for it in range(ITERS):
         for condition, copy in arrivals:
@@ -303,7 +308,7 @@
             for task, lag in zip(tasks, lags):
                 if 0 <= stage - lag < groups:
                     task(stage - lag)
-            if it == 0 and stage < groups:
+            if it == 0 and stage + 3 < len(plan):
                 part_weights(plan[2 + stage], plan[3 + stage])
             if it == 0 and stage == groups:
                 for copy in hin_copies:

time: 154 us -> 153 us (level)
  no operation moved by 1% of the time
where the time goes in v6:
time: 153 us; the launch traced here: 152 us
  Pallas kernels  146 us (95%)
  local copies, waits for them, and re-layouts  5.46 us (4%)
    pallas_call x1, Pallas kernels, fused_device(): pl.pallas_call(functools.partial(fused_kernel, n, zn), out_shape=(jax.Sha...  146 us
    unnamed x2, local copies, waits for them, and re-layouts  4.15 us

profile of v6, /device:TPU:0, one launch (start us, length us, event | category | flops | bytes accessed | tf_op | source)
XLA Modules:
  0.0 151.8 jit_solution(4694028460733278149)
XLA Ops:
  0.6 1.3 reshape.7.gain_ref
  1.9 145.7 %shard_map.77 = (f32[128,1024]{1,0:T(8,128)}, f32[128,2,1024]{2,1,0:T(2,128)}) custom-call(bf16[128,1024]{1,0:T(8,128)(2,1)} %q_ref.1, bf16[128,2,1024]{2,1,0:T(2,128)(2,1)} %kv_ref.1, bf16[128,1024]{1,0:T(8,128)(2,1)} %hin_ref.1, bf16[1,4096]{1,0:T(2,128)(2,1)} %reshape.7.gain_ref, bf16[1024,512]{1,0:T(8,128)(2,1)} %wout_ref.1, bf16[4096,2,1024]{2,1,0:T(2,128)(2,1)} %wkv_hbm.1), custom_call_target="tpu_custom_call" | custom-call | tf_op jit(solution)/shard_map/pallas_call | solution.py:344
  147.6 1.9 %copy.10 = f32[128,1024]{1,0:T(8,128)} copy(f32[128,1024]{1,0:T(8,128)} %get-tuple-element.4) | data formatting | bytes 1048576
  149.5 2.3 %copy.11 = f32[128,2,1024]{2,1,0:T(2,128)} copy(f32[128,2,1024]{2,1,0:T(2,128)} %get-tuple-element.5) | data formatting | bytes 2097152
